TPU v7x, 32 devices: a whole 2x2x4 slice. The times are simulated.
32 devices in a mesh: member: 8 (over z, y), fsdp: 4 (over x, core).
Axes of the slice: x: 2, y: 2, z: 4, core: 2. Of those that a mesh axis runs over, the one named last changes fastest.
Arguments:
- probe_acts: bfloat16 [8, 4, 224, 4096], P('member', 'fsdp'), may hold values from -6 to 6
- member_weight: bfloat16 [8, 4096, 1792], P('member', 'fsdp'), may hold values from -6 to 6
- gate_values: bfloat16 [8, 4, 224, 1792], P('member', 'fsdp'), may hold values from -6 to 6
- out_grad: bfloat16 [8, 4, 224, 1792], P('member', 'fsdp'), may hold values from -6 to 6
- loss_mask: int32 [4, 224], P('fsdp'), may hold values 0 or 1
Outputs:
- merged: bfloat16 [4096, 1792], P(None, 'member')
- fisher_mean: float32 [4096, 1792], P('fsdp', 'member')
All inputs are finite; a program needn't handle non-finite values. No bound on the sum of `loss_mask` on one device may be relied on, other than what follows from the above.
Results may differ from a plain program's by a relative error of at most 0.0045.
Values may be sent and summed in bfloat16 or wider, within the bound.
A program may use at most 128 MiB of HBM per device.

v0:
```python
import jax
import jax.numpy as jnp
from jax import lax
from jax.sharding import PartitionSpec as P


def shards(probe_acts, member_weight, gate_values, out_grad, loss_mask):
    acts_local = probe_acts[0]
    weight_shard = member_weight[0]
    own_rows = weight_shard.shape[0]
    width_cols = weight_shard.shape[1]
    seq_len = acts_local.shape[1]
    gate_act = jax.nn.silu(gate_values[0].astype(jnp.float32))
    mask_float = loss_mask.astype(jnp.float32)[:, :, None]
    cotangent = (mask_float * out_grad[0].astype(jnp.float32) * gate_act).astype(jnp.bfloat16)
    columns = lax.all_to_all(acts_local, "fsdp", split_axis=2, concat_axis=0, tiled=True)
    norm_factor = 1.0 / (columns.shape[0] * seq_len)
    zeros_block = jnp.zeros((own_rows, width_cols), jnp.float32)
    all_cotangents = lax.all_gather(cotangent, "fsdp", axis=0, tiled=True)

    def add_example(index, acc):
        acts_one = lax.dynamic_index_in_dim(columns, 0 + index, 0, keepdims=False)
        cot_one = lax.dynamic_index_in_dim(all_cotangents, index, 0, keepdims=False)
        grads = jnp.einsum("lr,lc->rc", acts_one, cot_one, preferred_element_type=jnp.float32)
        return acc + grads * grads

    squares = lax.fori_loop(0, all_cotangents.shape[0], add_example, zeros_block)
    fisher = squares * norm_factor
    weighted_term = fisher * weight_shard.astype(jnp.float32)
    share_cols = width_cols // lax.axis_size("member")
    total_full, weighted_full = lax.psum((fisher, weighted_term), "member")
    first_col = lax.axis_index("member") * share_cols
    fisher_total = lax.dynamic_slice_in_dim(total_full, first_col, share_cols, 1)
    weighted = lax.dynamic_slice_in_dim(weighted_full, first_col, share_cols, 1)
    merged_part = (weighted / (fisher_total + 1e-06)).astype(jnp.bfloat16)
    merged = lax.all_gather(merged_part, "fsdp", axis=0, tiled=True)
    fisher_mean = fisher_total / lax.axis_size("member")
    return (merged, fisher_mean)


def solution(mesh):
    in_specs = (
        P("member", "fsdp", None, None),
        P("member", "fsdp", None),
        P("member", "fsdp", None, None),
        P("member", "fsdp", None, None),
        P("fsdp", None),
    )
    out_specs = (P(None, "member"), P("fsdp", "member"))
    return jax.shard_map(shards, mesh=mesh, in_specs=in_specs, out_specs=out_specs, check_vma=False)
```

profile of v0, /device:TPU:0, one launch (start us, length us, event | category | flops | bytes accessed | tf_op | source)
XLA Modules:
  0.0 622.8 jit_solution(4245465798634222640)
XLA Ops:
  7.2 0.0 copy-start
  7.2 0.0 all-gather.3.cloned.1.call-start
  7.2 0.8 convert_element_type.53
  8.0 2.8 fusion.9
  10.9 0.0 all-gather.3.cloned.1.call-update
  10.9 0.0 copy-done
  10.9 8.6 %copy.17 = bf16[1,224,4096]{1,0,2:T(2,128)(2,1)} copy(bf16[1,224,4096]{2,1,0:T(8,128)(2,1)S(1)} %bitcast.31) | data formatting | bytes 3670016 | tf_op jit(solution)/shard_map/squeeze | solution.py:8
  19.5 0.5 broadcast.46
  20.0 23.7 %reduce = bf16[4096,224]{1,0:T(8,128)(2,1)S(1)} reduce(bf16[4096,1,224]{2,1,0:T(2,128)(2,1)} %bitcast.27, bf16[]{:T(256)} %broadcast.46), dimensions={1}, to_apply=%bitcast.21.reduce_sub_computation | reduce | bytes 3670018
  43.7 4.3 reshape.97
  48.0 4.2 all-to-all-start
  52.2 5.9 copy.21
  58.2 17.0 %all-to-all-done = bf16[4,2,114688]{2,1,0:T(2,128)(2,1)S(1)} async-done(((bf16[4,2,114688]{2,1,0:T(2,128)(2,1)}), bf16[4,2,114688]{2,1,0:T(2,128)(2,1)S(1)}, u32[]{:S(2)}, u32[]{:S(2)}) %all-to-all-start) | async-done | bytes 1835040 | tf_op jit(solution)/shard_map/all_to_all | solution.py:16
  75.2 5.2 reshape.98
  80.3 2.5 copy.23
  82.9 2.4 copy.22
  85.3 2.0 copy.19
  87.3 0.0 all-gather.3.cloned.1.call-done
  87.4 27.7 %while.14 = (s32[]{:T(128)}, f32[1024,1792]{1,0:T(8,128)}, bf16[4,224,1024]{2,1,0:T(8,128)(2,1)S(1)}, bf16[4,224,1792]{2,1,0:T(8,128)(2,1)}, s32[]{:T(128)}, /*index=5*/s32[]{:T(128)}) while((s32[]{:T(128)}, f32[1024,1792]{1,0:T(8,128)}, bf16[4,224,1024]{2,1,0:T(8,128)(2,1)S(1)}, bf16[4,224,1792]{2,1,0:T(8,128)(2,1)}, s32[]{:T(128)}, ...), condition=%wide.region_1.2_spmd.clone, body=%wide.region_0.1_spmd.clone.sunk | while | flops 827588608 | bytes 15943254 | solution.py:27
  87.4 5.3 select_add_fusion.2
  92.7 7.5 %select_add_fusion.2 = f32[1024,1792]{1,0:T(8,128)} fusion(f32[1024,1792]{1,0:T(8,128)} %get-tuple-element.155, pred[]{:T(512)S(6)} %compare.3, bf16[4,224,1792]{2,1,0:T(8,128)(2,1)} %get-tuple-element.163, s32[]{:T(128)S(6)} %copy.26, bf16[4,224,1024]{2,1,0:T(8,128)(2,1)S(1)} %get-tuple-element.162), kind=kOutput, calls=%fused_computation.clone.1 | convolution fusion | flops 827588608 | bytes 15943168 | tf_op jit(solution)/shard_map/while/body/eval_jaxpr/lr,lc->rc/dot_general | solution.py:24
  100.1 7.5 %select_add_fusion.2 = f32[1024,1792]{1,0:T(8,128)} fusion(f32[1024,1792]{1,0:T(8,128)} %get-tuple-element.155, pred[]{:T(512)S(6)} %compare.3, bf16[4,224,1792]{2,1,0:T(8,128)(2,1)} %get-tuple-element.163, s32[]{:T(128)S(6)} %copy.26, bf16[4,224,1024]{2,1,0:T(8,128)(2,1)S(1)} %get-tuple-element.162), kind=kOutput, calls=%fused_computation.clone.1 | convolution fusion | flops 827588608 | bytes 15943168 | tf_op jit(solution)/shard_map/while/body/eval_jaxpr/lr,lc->rc/dot_general | solution.py:24
  107.6 7.5 %select_add_fusion.2 = f32[1024,1792]{1,0:T(8,128)} fusion(f32[1024,1792]{1,0:T(8,128)} %get-tuple-element.155, pred[]{:T(512)S(6)} %compare.3, bf16[4,224,1792]{2,1,0:T(8,128)(2,1)} %get-tuple-element.163, s32[]{:T(128)S(6)} %copy.26, bf16[4,224,1024]{2,1,0:T(8,128)(2,1)S(1)} %get-tuple-element.162), kind=kOutput, calls=%fused_computation.clone.1 | convolution fusion | flops 827588608 | bytes 15943168 | tf_op jit(solution)/shard_map/while/body/eval_jaxpr/lr,lc->rc/dot_general | solution.py:24
  115.1 8.4 %copy.20 = f32[1024,1792]{0,1:T(8,128)} copy(f32[1024,1792]{1,0:T(8,128)} %get-tuple-element.81) | data formatting | bytes 14680064 | tf_op jit(solution)/shard_map/while | solution.py:27
  123.5 12.1 %broadcast_multiply_fusion = (f32[1024,1792]{0,1:T(8,128)}, f32[1024,1792]{0,1:T(8,128)}) fusion(f32[1024,1792]{0,1:T(8,128)} %copy.20, bf16[1,1024,1792]{1,2,0:T(8,128)(2,1)} %copy.21), kind=kLoop, calls=%fused_computation.7 | loop fusion | flops 5505024 | bytes 25690112 | tf_op jit(solution)/shard_map/mul | solution.py:28
  135.6 0.0 all-reduce.3.cloned.1.call-update
  135.6 0.0 all-gather.5.cloned.1.call-start
  135.7 454.5 %all-reduce.3.cloned.1.call-done = (f32[1024,1792]{0,1:T(8,128)}, f32[1024,1792]{0,1:T(8,128)}) async-done(((f32[1024,1792]{0,1:T(8,128)}, f32[1024,1792]{0,1:T(8,128)}), (f32[1024,1792]{0,1:T(8,128)}, f32[1024,1792]{0,1:T(8,128)})) %all-reduce.3.cloned.1.call-update) | async-done | bytes 14680080 | tf_op jit(solution)/shard_map/psum | solution.py:31
  590.2 2.8 dynamic-slice_multiply_fusion
  593.0 0.0 all-gather.5.cloned.1.call-update
  593.0 20.3 %all-gather.5.cloned.1.call-done = bf16[4096,224]{0,1:T(8,128)(2,1)} async-done(((bf16[1024,224]{0,1:T(8,128)(2,1)}), bf16[4096,224]{0,1:T(8,128)(2,1)}) %all-gather.5.cloned.1.call-update) | async-done | bytes 1835024 | tf_op jit(solution)/shard_map/all_gather | solution.py:36
  613.3 2.9 copy.33
  (2 shorter events, 0.0 us)
Async XLA Ops:
  7.2 3.7 copy-start
  7.2 80.2 %all-gather.3.cloned.1.call-start = ((), (), s32[]{:S(2)}) async-start(), calls=%async_computation.1 | async-start | bytes 4014080 | tf_op jit(solution)/shard_map/all_gather | solution.py:19
  48.0 27.2 %all-to-all-start = ((bf16[4,2,114688]{2,1,0:T(2,128)(2,1)}), bf16[4,2,114688]{2,1,0:T(2,128)(2,1)S(1)}, u32[]{:S(2)}, u32[]{:S(2)}) async-start(bf16[4,2,114688]{2,1,0:T(2,128)(2,1)} %reshape.97), calls=%async_computation | async-start | bytes 3670016 | tf_op jit(solution)/shard_map/all_to_all | solution.py:16
  52.2 538.0 %all-reduce.3.cloned.1.call-start = ((), (), s32[]{:S(2)}) async-start(), calls=%async_computation.3 | async-start | bytes 29360128 | tf_op jit(solution)/shard_map/psum | solution.py:31
  135.6 477.7 %all-gather.5.cloned.1.call-start = ((), (), s32[]{:S(2)}) async-start(), calls=%async_computation.2 | async-start | bytes 2293760 | tf_op jit(solution)/shard_map/all_gather | solution.py:36
Sparse Core Ops, SparseCore 0:
  11.0 31.5 all-gather.2
  135.8 454.4 all-reduce.2
  593.1 20.1 all-gather.4
where the time goes:
time: 623 us
  waiting for transfers between devices  492 us (79%)
  local copies, waits for them, and re-layouts  42.8 us (7%)
  other arithmetic  42.2 us (7%)
  matrix products  27.7 us (4%)
  between operations  13.8 us (2%)
    psum x1, waiting for transfers between devices, shards(): total_full, weighted_full = lax.psum((fisher, weighted_term), 'member')  455 us
    dot_general x4, matrix products, add_example(): jnp.einsum('lr,lc->rc', acts_one, cot_one, preferred_element_type=jnp.flo...  27.7 us
    unnamed x2, other arithmetic  23.7 us
    unnamed x9, local copies, waits for them, and re-layouts  23.5 us
    all_gather x1, waiting for transfers between devices, shards(): merged = lax.all_gather(merged_part, 'fsdp', axis=0, tiled=True)  20.3 us
    all_to_all x1, waiting for transfers between devices, shards(): lax.all_to_all(acts_local, 'fsdp', split_axis=2, concat_axis=0, tiled=True)  17 us
  transfers between devices with their start and end apart: 4, of which 3 were waited for; matrix products, arithmetic and copies ran while one was open for 9% of the time, Pallas kernels for 0%

commit v1 on v0

v1 whole, which is shorter than its diff:
```python
import functools

import jax
import jax.numpy as jnp
from jax import lax
from jax.experimental import pallas as pl
from jax.experimental.pallas import tpu as pltpu
from jax.sharding import PartitionSpec as P

MESH = pl.DeviceIdType.MESH
F32 = jnp.float32
BF16 = jnp.bfloat16


def merge_kernel(
    F, M, C, acts_hbm, w_hbm, gate, grad, mask, merged_out, fisher_out,
    acts, cots, cot_t, w, w_t, ysend, yrecv, zsend, zrecv, own, fin, fmean,
    acts_ss, acts_rs, acts_ls, cot_ss, cot_rs, w_ls, y_ss, y_rs, z_ss, z_rs, fin_ss, fin_rs, out_ls,
):
    f = lax.axis_index("fsdp")
    m = lax.axis_index("member")
    Z = M // 2
    z = lax.div(m, 2)
    y = lax.rem(m, 2)
    L = cots.shape[2]
    H = cots.shape[3]
    COLS = 2 * H
    S = COLS // M
    CH = acts.shape[3]
    R = C * CH
    norm = 1.0 / (F * L)
    mate = f + 1 - 2 * lax.rem(f, 2)
    m_y = m + 1 - 2 * y

    def peer(d):
        return lax.rem(f + d, F)

    barrier = pltpu.get_barrier_semaphore()
    for d in range(1, F):
        pl.semaphore_signal(barrier, inc=1, device_id=(m, peer(d)), device_id_type=MESH)
    pl.semaphore_signal(barrier, inc=1, device_id=(m_y, f), device_id_type=MESH)

    @pl.when(z > 0)
    def _():
        pl.semaphore_signal(barrier, inc=1, device_id=(m - 2, f), device_id_type=MESH)

    @pl.when(z < Z - 1)
    def _():
        pl.semaphore_signal(barrier, inc=1, device_id=(m + 2, f), device_id_type=MESH)

    w_copy = pltpu.make_async_copy(w_hbm, w, w_ls)
    w_copy.start()

    def own_acts(c):
        start = pl.multiple_of(f * R + c * CH, 128)
        return pltpu.make_async_copy(acts_hbm.at[:, pl.ds(start, CH)], acts.at[c, f], acts_ls.at[c])

    for c in range(C):
        own_acts(c).start()

    def acts_copy(d, c):
        p = peer(d)
        start = pl.multiple_of(p * R + c * CH, 128)
        return pltpu.make_async_remote_copy(
            src_ref=acts_hbm.at[:, pl.ds(start, CH)], dst_ref=acts.at[c, f],
            send_sem=acts_ss.at[d - 1, c], recv_sem=acts_rs.at[f, c],
            device_id=(m, p), device_id_type=MESH)

    def acts_arrival(d, c):
        s = peer(d)
        return pltpu.make_async_remote_copy(
            src_ref=acts.at[c, s], dst_ref=acts.at[c, s],
            send_sem=acts_ss.at[d - 1, c], recv_sem=acts_rs.at[s, c],
            device_id=(m, s), device_id_type=MESH)

    def cot_copy(s, h, p, slot):
        return pltpu.make_async_remote_copy(
            src_ref=cots.at[h, s], dst_ref=cots.at[h, s],
            send_sem=cot_ss.at[slot, h], recv_sem=cot_rs.at[s, h],
            device_id=(m, p), device_id_type=MESH)

    lower = z < Z // 2
    first = jnp.where(lower, 1, 0)
    second = 1 - first

    mask_col = jnp.transpose(jnp.broadcast_to(mask[...].astype(F32), (128, L)))

    def make_cot(h):
        for t in range(H // 128):
            cols = pl.ds(pl.multiple_of(h * H + t * 128, 128), 128)
            g = gate[:, cols].astype(F32)
            value = mask_col * grad[:, cols].astype(F32) * (g / (1.0 + jnp.exp(-g)))
            cots[h, f, :, t * 128:(t + 1) * 128] = value.astype(BF16)

    def send_cot(h):
        for d in range(2, F, 2):
            cot_copy(f, h, peer(d), d).start()
        cot_copy(f, h, mate, 0).start()

    make_cot(first)
    pl.semaphore_wait(barrier, F + jnp.where(z > 0, 1, 0) + jnp.where(z < Z - 1, 1, 0))

    send_cot(first)
    for d in range(1, F):
        acts_copy(d, 0).start()
    make_cot(second)
    send_cot(second)
    for c in range(1, C):
        for d in range(1, F):
            acts_copy(d, c).start()

    w_copy.wait()

    def turn_weight(c, carry):
        rows = pl.ds(pl.multiple_of(c * CH, CH), CH)
        for t in range(COLS // 128):
            tile = w[rows, t * 128:(t + 1) * 128].astype(F32)
            w_t[c, t * 128:(t + 1) * 128, :] = jnp.transpose(tile)
        return carry

    lax.fori_loop(0, C, turn_weight, 0)

    def relay(h):
        for d in range(2, F, 2):
            s = peer(d)
            cot_copy(s, h, s, d).wait_recv()
            cot_copy(s, h, mate, d + 1).start()

    def turn_cot(h):
        for d in range(1, F, 2):
            s = peer(d)
            cot_copy(s, h, s, d).wait_recv()

        def one(e, carry):
            for t in range(H // 128):
                tile = cots[h, e, :, t * 128:(t + 1) * 128].astype(F32)
                rows = pl.ds(pl.multiple_of(h * H + t * 128, 128), 128)
                cot_t[e, rows, :] = jnp.transpose(tile)
            return carry

        lax.fori_loop(0, F, one, 0)

    relay(first)

    def share(j, c):
        rows = pl.ds(pl.multiple_of(j * S, 8), S)
        squares = None
        for e in range(F):
            g = jnp.dot(cot_t[e, rows, :].astype(BF16), acts[c, e], preferred_element_type=F32)
            squares = g * g if squares is None else squares + g * g
        fisher = squares * norm
        return fisher, fisher * w_t[c, rows, :]

    def y_copy(c, k):
        return pltpu.make_async_remote_copy(
            src_ref=ysend.at[c, k], dst_ref=yrecv.at[c, k],
            send_sem=y_ss.at[c, k], recv_sem=y_rs.at[c, k],
            device_id=(m_y, f), device_id_type=MESH)

    def z_copy(c, k, slot, target):
        return pltpu.make_async_remote_copy(
            src_ref=zsend.at[c, k], dst_ref=zrecv.at[c, slot],
            send_sem=z_ss.at[c, k], recv_sem=z_rs.at[c, slot],
            device_id=(target, f), device_id_type=MESH)

    def fin_copy(c, d):
        return pltpu.make_async_remote_copy(
            src_ref=fin.at[c], dst_ref=merged_out.at[f, :, pl.ds(pl.multiple_of(c * CH, CH), CH)],
            send_sem=fin_ss.at[d, c], recv_sem=fin_rs.at[f, c],
            device_id=(m, peer(d)), device_id_type=MESH)

    def fin_arrival(c, d):
        s = peer(d)
        return pltpu.make_async_remote_copy(
            src_ref=fin.at[c], dst_ref=merged_out.at[s, :, pl.ds(pl.multiple_of(c * CH, CH), CH)],
            send_sem=fin_ss.at[d, c], recv_sem=fin_rs.at[s, c],
            device_id=(m, s), device_id_type=MESH)

    def out_copies(c):
        cols = pl.ds(pl.multiple_of(c * CH, CH), CH)
        return (
            pltpu.make_async_copy(fin.at[c], merged_out.at[f, :, cols], out_ls.at[0, c]),
            pltpu.make_async_copy(fmean.at[c], fisher_out.at[:, cols], out_ls.at[1, c]),
        )

    def combine(c, k):
        b = lax.rem(c, 2)
        y_copy(c, k).wait_recv()
        own[b, k] = own[b, k] + yrecv[c, k].astype(F32)

        @pl.when((z > 0) & (k >= z))
        def _():
            z_copy(c, k, k, m_y).wait_recv()
            own[b, k] = own[b, k] + zrecv[c, k].astype(F32)

        @pl.when((z < Z - 1) & (k <= z))
        def _():
            slot = jnp.where(k == z, Z, k)
            z_copy(c, k, slot, m_y).wait_recv()
            own[b, k] = own[b, k] + zrecv[c, slot].astype(F32)

        @pl.when(k != z)
        def _():
            zsend[c, k] = own[b, k].astype(BF16)

        @pl.when(k > z)
        def _():
            z_copy(c, k, k, m + 2).start()

        @pl.when(k < z)
        def _():
            z_copy(c, k, jnp.where(k == z - 1, Z, k), m - 2).start()

        @pl.when(k == z)
        def _():
            total = own[b, k, 0]
            fin[c] = (own[b, k, 1] / (total + 1e-6)).astype(BF16)
            fmean[c] = total * (1.0 / M)
            for d in range(1, F):
                fin_copy(c, d).start()
            for copy in out_copies(c):
                copy.start()

    def order(i):
        return jnp.where(lower, Z - 1 - i, i)

    def step(t, carry):
        c = lax.div(t, Z)
        i = lax.rem(t, Z)
        k = order(i)

        @pl.when(t == 0)
        def _():
            turn_cot(first)

        @pl.when(t == 1)
        def _():
            relay(second)

        @pl.when(t == Z // 2)
        def _():
            turn_cot(second)

        @pl.when((i == 0) & (c < C))
        def _():
            own_acts(c).wait()
            for d in range(1, F):
                acts_arrival(d, c).wait_recv()

        @pl.when(c < C)
        def _():
            fisher, weighted = share(2 * k + 1 - y, c)
            ysend[c, k, 0] = fisher.astype(BF16)
            ysend[c, k, 1] = weighted.astype(BF16)
            y_copy(c, k).start()

        @pl.when(c > 0)
        def _():
            combine(c - 1, k)

        @pl.when(c < C)
        def _():
            fisher, weighted = share(2 * k + y, c)
            b = lax.rem(c, 2)
            own[b, k, 0] = fisher
            own[b, k, 1] = weighted

        return carry

    lax.fori_loop(0, (C + 1) * Z, step, 0)

    for h in range(2):
        for slot in [0] + [s for d in range(2, F, 2) for s in (d, d + 1)]:
            cot_copy(f, h, mate, slot).wait_send()

    def drain(c, carry):
        for d in range(1, F):
            acts_copy(d, c).wait_send()
            fin_copy(c, d).wait_send()
            fin_arrival(c, d).wait_recv()
        for copy in out_copies(c):
            copy.wait()

        def drain_k(k, carry):
            y_copy(c, k).wait_send()

            @pl.when(k != z)
            def _():
                z_copy(c, k, k, m_y).wait_send()

            return carry

        return lax.fori_loop(0, Z, drain_k, carry)

    lax.fori_loop(0, C, drain, 0)


def shards(F, M, probe_acts, member_weight, gate_values, out_grad, loss_mask):
    acts = probe_acts[0, 0]
    weight = member_weight[0]
    gate = gate_values[0, 0]
    grad = out_grad[0, 0]
    L, D = acts.shape
    R, COLS = weight.shape
    S = COLS // M
    Z = M // 2
    CH = max(128, R // 4)
    C = R // CH
    dma = pltpu.SemaphoreType.DMA
    vmem = pl.BlockSpec(memory_space=pltpu.VMEM)
    hbm = pl.BlockSpec(memory_space=pl.ANY)
    merged, fisher = pl.pallas_call(
        functools.partial(merge_kernel, F, M, C),
        out_shape=(
            jax.ShapeDtypeStruct((F, S, R), BF16),
            jax.ShapeDtypeStruct((S, R), F32),
        ),
        in_specs=[hbm, hbm, vmem, vmem, vmem],
        out_specs=(hbm, hbm),
        scratch_shapes=[
            pltpu.VMEM((C, F, L, CH), BF16),
            pltpu.VMEM((2, F, L, COLS // 2), BF16),
            pltpu.VMEM((F, COLS, L), F32),
            pltpu.VMEM((R, COLS), BF16),
            pltpu.VMEM((C, COLS, CH), F32),
            pltpu.VMEM((C, Z, 2, S, CH), BF16),
            pltpu.VMEM((C, Z, 2, S, CH), BF16),
            pltpu.VMEM((C, Z, 2, S, CH), BF16),
            pltpu.VMEM((C, Z + 1, 2, S, CH), BF16),
            pltpu.VMEM((2, Z, 2, S, CH), F32),
            pltpu.VMEM((C, S, CH), BF16),
            pltpu.VMEM((C, S, CH), F32),
            dma((F, C)), dma((F, C)), dma((C,)),
            dma((F, 2)), dma((F, 2)), dma,
            dma((C, Z)), dma((C, Z)),
            dma((C, Z)), dma((C, Z + 1)),
            dma((F, C)), dma((F, C)), dma((2, C)),
        ],
        compiler_params=pltpu.CompilerParams(
            collective_id=0, has_side_effects=True, vmem_limit_bytes=60 * 1024 * 1024),
        cost_estimate=pl.CostEstimate(
            flops=2 * F * L * R * COLS, bytes_accessed=2 * R * COLS, transcendentals=L * COLS),
    )(acts, weight, gate, grad, loss_mask)
    merged = jnp.transpose(merged, (0, 2, 1)).reshape(F * R, S)
    return merged, jnp.transpose(fisher)


def solution(mesh):
    in_specs = (
        P("member", "fsdp", None, None),
        P("member", "fsdp", None),
        P("member", "fsdp", None, None),
        P("member", "fsdp", None, None),
        P("fsdp", None),
    )
    out_specs = (P(None, "member"), P("fsdp", "member"))
    body = functools.partial(shards, mesh.shape["fsdp"], mesh.shape["member"])
    return jax.shard_map(body, mesh=mesh, in_specs=in_specs, out_specs=out_specs, check_vma=False)
```

time: 623 us -> 143 us (0.23)
  waiting for transfers between devices: 492 us -> 0 us
  Pallas kernels: 0 us -> 137 us
  other arithmetic: 42.2 us -> 0 us
  local copies, waits for them, and re-layouts: 42.8 us -> 3.94 us
  matrix products: 27.7 us -> 0 us
  between operations: 13.8 us -> 0.65 us
    psum x1 -> x0, waiting for transfers between devices: 455 us -> none  [shards(): total_full, weighted_full = lax.psum((fisher, weighted_term), 'member')]
    pallas_call x0 -> x1, Pallas kernels: none -> 137 us  [shards(): pl.pallas_call(functools.partial(merge_kernel, F, M, C), out_shape=(jax.S...]
    dot_general x4 -> x0, matrix products: 27.7 us -> none  [add_example(): jnp.einsum('lr,lc->rc', acts_one, cot_one, preferred_element_type=jnp.flo...]
    unnamed x2 -> x0, other arithmetic: 23.7 us -> none
    unnamed x9 -> x3, local copies, waits for them, and re-layouts: 23.5 us -> 0.93 us
    all_gather x2 -> x0, waiting for transfers between devices: 20.3 us -> none  [the longest x1 20.3 us: shards(): merged = lax.all_gather(merged_part, 'fsdp', axis=0, tiled=True)]
    all_to_all x1 -> x0, waiting for transfers between devices: 17 us -> none  [shards(): lax.all_to_all(acts_local, 'fsdp', split_axis=2, concat_axis=0, tiled=True)]
    mul x1 -> x0, other arithmetic: 12.1 us -> none  [shards(): fisher = squares * norm_factor]
  transfers between devices with their start and end apart: 4 -> 0, of which waited for: 3 -> 0; matrix products, arithmetic and copies ran while one was open for 9% -> 0% of each run, Pallas kernels for 0% -> 0%
where the time goes in v1:
time: 143 us; the launch traced here: 142 us
  Pallas kernels  137 us (96%)
  local copies, waits for them, and re-layouts  3.94 us (3%)
    pallas_call x1, Pallas kernels, shards(): pl.pallas_call(functools.partial(merge_kernel, F, M, C), out_shape=(jax.S...  137 us
    reshape x1, local copies, waits for them, and re-layouts, shards(): merged = jnp.transpose(merged, (0, 2, 1)).reshape(F * R, S)  3.01 us

profile of v1, /device:TPU:0, one launch (start us, length us, event | category | flops | bytes accessed | tf_op | source)
XLA Modules:
  0.0 141.9 jit_solution(17852453280835511457)
XLA Ops:
  0.6 137.3 %shard_map.68 = (bf16[4,224,1024]{2,1,0:T(8,128)(2,1)}, f32[224,1024]{1,0:T(8,128)}) custom-call(bf16[224,4096]{1,0:T(8,128)(2,1)} %bitcast.12, bf16[1024,1792]{1,0:T(8,128)(2,1)} %bitcast.11, bf16[224,1792]{1,0:T(8,128)(2,1)} %bitcast.13, bf16[224,1792]{1,0:T(8,128)(2,1)} %bitcast.14, s32[1,224]{1,0:T(1,128)} %mask.1), custom_call_target="tpu_custom_call" | custom-call | flops 3288334336 | bytes 3670016 | tf_op jit(solution)/shard_map/pallas_call | solution.py:312
  137.9 0.0 copy-start
  137.9 3.0 %copy.8 = bf16[4,28,8,1024]{3,2,0,1:T(8,128)(2,1)} copy(bf16[4,28,8,1024]{3,2,1,0:T(8,128)(2,1)} %bitcast.9) | data formatting | bytes 3670016 | tf_op jit(solution)/shard_map/reshape | solution.py:344
  141.0 0.0 copy-done
  141.0 0.9 copy.10
Async XLA Ops:
  137.9 3.0 %copy-start = (f32[224,1024]{1,0:T(8,128)S(1)}, f32[224,1024]{1,0:T(8,128)}, u32[]{:S(2)}) copy-start(f32[224,1024]{1,0:T(8,128)} %get-tuple-element.5) | copy-start | bytes 2752516

commit v2 on v1

--- a/solution.py
+++ b/solution.py
@@ -10,6 +10,7 @@
 MESH = pl.DeviceIdType.MESH
 F32 = jnp.float32
 BF16 = jnp.bfloat16
+LAG = 3
 
 
 def merge_kernel(
@@ -254,10 +255,6 @@
             ysend[c, k, 1] = weighted.astype(BF16)
             y_copy(c, k).start()
 
-        @pl.when(c > 0)
-        def _():
-            combine(c - 1, k)
-
         @pl.when(c < C)
         def _():
             fisher, weighted = share(2 * k + y, c)
@@ -265,9 +262,20 @@
             own[b, k, 0] = fisher
             own[b, k, 1] = weighted
 
+        @pl.when(t >= LAG)
+        def _():
+            late = t - LAG
+            k_late = order(lax.rem(late, Z))
+            c_late = lax.div(late, Z) - jnp.where(k_late == z, 1, 0)
+
+            @pl.when(c_late >= 0)
+            def _():
+                combine(c_late, k_late)
+
         return carry
 
-    lax.fori_loop(0, (C + 1) * Z, step, 0)
+    lax.fori_loop(0, C * Z + LAG, step, 0)
+    combine(C - 1, z)
 
     for h in range(2):
         for slot in [0] + [s for d in range(2, F, 2) for s in (d, d + 1)]:

time: 143 us -> 122 us (0.85)
  Pallas kernels: 137 us -> 117 us
    pallas_call x1, Pallas kernels: 137 us -> 117 us  [shards(): pl.pallas_call(functools.partial(merge_kernel, F, M, C), out_shape=(jax.S...]
where the time goes in v2:
time: 122 us
  Pallas kernels  117 us (96%)
  local copies, waits for them, and re-layouts  3.94 us (3%)
    pallas_call x1, Pallas kernels, shards(): pl.pallas_call(functools.partial(merge_kernel, F, M, C), out_shape=(jax.S...  117 us
    reshape x1, local copies, waits for them, and re-layouts, shards(): merged = jnp.transpose(merged, (0, 2, 1)).reshape(F * R, S)  3.01 us

profile of v2, /device:TPU:0, one launch (start us, length us, event | category | flops | bytes accessed | tf_op | source)
XLA Modules:
  0.0 121.6 jit_solution(16529730560297879595)
XLA Ops:
  0.6 117.0 %shard_map.68 = (bf16[4,224,1024]{2,1,0:T(8,128)(2,1)}, f32[224,1024]{1,0:T(8,128)}) custom-call(bf16[224,4096]{1,0:T(8,128)(2,1)} %bitcast.12, bf16[1024,1792]{1,0:T(8,128)(2,1)} %bitcast.11, bf16[224,1792]{1,0:T(8,128)(2,1)} %bitcast.13, bf16[224,1792]{1,0:T(8,128)(2,1)} %bitcast.14, s32[1,224]{1,0:T(1,128)} %mask.1), custom_call_target="tpu_custom_call" | custom-call | flops 3288334336 | bytes 3670016 | tf_op jit(solution)/shard_map/pallas_call | solution.py:320
  117.6 0.0 copy-start
  117.6 3.0 %copy.8 = bf16[4,28,8,1024]{3,2,0,1:T(8,128)(2,1)} copy(bf16[4,28,8,1024]{3,2,1,0:T(8,128)(2,1)} %bitcast.9) | data formatting | bytes 3670016 | tf_op jit(solution)/shard_map/reshape | solution.py:352
  120.7 0.0 copy-done
  120.7 0.9 copy.10
Async XLA Ops:
  117.6 3.0 %copy-start = (f32[224,1024]{1,0:T(8,128)S(1)}, f32[224,1024]{1,0:T(8,128)}, u32[]{:S(2)}) copy-start(f32[224,1024]{1,0:T(8,128)} %get-tuple-element.5) | copy-start | bytes 2752516
